TPU v7x, 32 devices: a whole 2x2x4 slice. The times are simulated.
32 devices in a mesh: dp: 4 (over x, core), mp: 8 (over z, y).
Axes of the slice: x: 2, y: 2, z: 4, core: 2. Of those that a mesh axis runs over, the one named last changes fastest.
Arguments:
- tokens: bfloat16 [4704, 768], P(('dp', 'mp')), may hold values from -6 to 6
- crop_kind: int32 [96], P('dp'), may hold values from 0 to 1, as said below
- norm1_gain: float32 [768], replicated, may hold values from 0.1 to 1.9
- norm1_bias: float32 [768], replicated, may hold values from -1.75 to 1.75
- qkv_weight: bfloat16 [3, 768, 768], P(None, None, 'mp'), may hold values from -0.21875 to 0.21875
- qv_bias: float32 [2, 768], P(None, 'mp'), may hold values from -3 to 3
- rel_table: float32 [169, 24], P(None, 'mp'), may hold values from -6 to 6
- proj_weight: bfloat16 [768, 768], P('mp'), may hold values from -0.875 to 0.875
- proj_bias: float32 [768], replicated, may hold values from -1.75 to 1.75
- norm2_gain: float32 [768], replicated, may hold values from 0.1 to 1.9
- norm2_bias: float32 [768], replicated, may hold values from -1.75 to 1.75
- fc1_weight: bfloat16 [768, 3072], P(None, 'mp'), may hold values from -0.21875 to 0.21875
- fc1_bias: float32 [3072], P('mp'), may hold values from -3 to 3
- fc2_weight: bfloat16 [3072, 768], P('mp'), may hold values from -0.109375 to 0.109375
- fc2_bias: float32 [768], replicated, may hold values from -1.75 to 1.75
- out_grad: bfloat16 [4704, 768], P(('dp', 'mp')), may hold values from -6 to 6
Outputs:
- block_out: bfloat16 [4704, 768], P(('dp', 'mp'))
- tokens_grad: bfloat16 [4704, 768], P(('dp', 'mp'))
- norm1_gain_grad: float32 [768], replicated
- norm1_bias_grad: float32 [768], replicated
- qkv_weight_grad: float32 [3, 768, 768], P(None, None, 'mp')
- qv_bias_grad: float32 [2, 768], P(None, 'mp')
- rel_table_grad: float32 [169, 24], P(None, 'mp')
- proj_weight_grad: float32 [768, 768], P('mp')
- proj_bias_grad: float32 [768], replicated
- norm2_gain_grad: float32 [768], replicated
- norm2_bias_grad: float32 [768], replicated
- fc1_weight_grad: float32 [768, 3072], P(None, 'mp')
- fc1_bias_grad: float32 [3072], P('mp')
- fc2_weight_grad: float32 [3072, 768], P('mp')
- fc2_bias_grad: float32 [768], replicated
Inputs may be any that keep to these rules, and one draw needn't show every extreme that they name: `crop_kind`: 0 marks a global crop, whose 49 slots all hold patches; 1 marks a local crop, whose first 9 slots hold patches. Both kinds occur.
All inputs are finite; a program needn't handle non-finite values.
Results may differ from a plain program's by a relative error of at most 0.024.
Values may be sent and summed in bfloat16 or wider, within the bound.
A program may use at most 64 MiB of HBM per device.

v0:
```python
import jax
import jax.numpy as jnp
from jax import lax
from jax.sharding import PartitionSpec as P

HEAD = 32
SIDE = 7
LOCAL_SIDE = 3
WIN = 49
EPSILON = 1e-05
NEG_FILL = -1000000000.0
HIGHEST = lax.Precision.HIGHEST


def normalize(values, gain_vec, shift_vec):
    centre = values - jnp.mean(values, axis=-1, keepdims=True)
    spread = jnp.mean(centre * centre, axis=-1, keepdims=True)
    return centre * lax.rsqrt(spread + EPSILON) * gain_vec + shift_vec


def gelu_tanh(values):
    return jax.nn.gelu(values, approximate=True)


def relative_index(side_len):
    slot_ids = jnp.minimum(jnp.arange(WIN), side_len * side_len - 1)
    slot_row = slot_ids // side_len
    slot_col = slot_ids % side_len
    offset_row = slot_row[:, None] - slot_row[None, :] + SIDE - 1
    offset_col = slot_col[:, None] - slot_col[None, :] + SIDE - 1
    return offset_row * (2 * SIDE - 1) + offset_col


def window_live(kinds):
    return jnp.where(kinds == 0, WIN, LOCAL_SIDE * LOCAL_SIDE)


def table_onehot():
    index_both = jnp.stack([relative_index(SIDE), relative_index(LOCAL_SIDE)]).reshape(2, WIN * WIN)
    entries = jnp.arange((2 * SIDE - 1) ** 2, dtype=jnp.int32)
    return (index_both[:, :, None] == entries[None, None, :]).astype(jnp.float32)


def dot_rows(left, right):
    return lax.dot_general(
        left, right, (((0,), (0,)), ((), ())), preferred_element_type=jnp.float32
    )


def dot_back(left, right):
    return lax.dot_general(
        left, right, (((1,), (1,)), ((), ())), preferred_element_type=jnp.float32
    )


def attention_scores(query_four, key_four, bias_win, key_usable):
    score_raw = jnp.einsum(
        "wqhd,wkhd->whqk", query_four, key_four, preferred_element_type=jnp.float32
    )
    return jnp.where(key_usable[:, None, None, :], score_raw + bias_win, NEG_FILL)


def forward_pass(inputs, kinds, row_live, params, onehot):
    (
        gain_one,
        shift_one,
        qkv_weight,
        qv_bias,
        rel_table,
        proj_weight,
        proj_bias,
        gain_two,
        shift_two,
        fc1_weight,
        fc1_bias,
        fc2_weight,
        fc2_bias,
    ) = params
    head_cols = qkv_weight.shape[2]
    heads_here = head_cols // HEAD
    windows = kinds.shape[0]
    normed_one = normalize(inputs, gain_one, shift_one).astype(jnp.bfloat16)
    rows_one = lax.all_gather(normed_one, "mp", axis=0, tiled=True)
    query_rows = (
        (jnp.dot(rows_one, qkv_weight[0], preferred_element_type=jnp.float32) + qv_bias[0])
        * HEAD ** (-0.5)
    ).astype(jnp.bfloat16)
    key_rows = jnp.dot(rows_one, qkv_weight[1], preferred_element_type=jnp.float32).astype(
        jnp.bfloat16
    )
    value_rows = (
        jnp.dot(rows_one, qkv_weight[2], preferred_element_type=jnp.float32) + qv_bias[1]
    ).astype(jnp.bfloat16)
    bias_both = jnp.einsum("kpt,th->khp", onehot, rel_table, precision=HIGHEST).reshape(
        2, heads_here, WIN, WIN
    )
    is_global = (kinds == 0)[:, None, None, None]
    bias_win = jnp.where(is_global, bias_both[0][None], bias_both[1][None])
    key_usable = jnp.arange(WIN)[None, :] < window_live(kinds)[:, None]
    win_shape = (windows, WIN, heads_here, HEAD)
    scores = attention_scores(
        query_rows.reshape(win_shape), key_rows.reshape(win_shape), bias_win, key_usable
    )
    row_max = jnp.max(scores, axis=-1, keepdims=True)
    log_total = row_max + jnp.log(jnp.sum(jnp.exp(scores - row_max), axis=-1, keepdims=True))
    prob_bf = jnp.exp(scores - log_total).astype(jnp.bfloat16)
    head_out = (
        jnp.einsum(
            "whqk,wkhd->wqhd",
            prob_bf,
            value_rows.reshape(win_shape),
            preferred_element_type=jnp.float32,
        )
        .reshape(windows * WIN, head_cols)
        .astype(jnp.bfloat16)
    )
    attn_branch = lax.psum_scatter(
        jnp.dot(head_out, proj_weight, preferred_element_type=jnp.float32).astype(jnp.bfloat16),
        "mp",
        scatter_dimension=0,
        tiled=True,
    ).astype(jnp.float32)
    middle = inputs + (attn_branch + proj_bias) * row_live
    normed_two = normalize(middle, gain_two, shift_two).astype(jnp.bfloat16)
    rows_two = lax.all_gather(normed_two, "mp", axis=0, tiled=True)
    hidden_pre = jnp.dot(rows_two, fc1_weight, preferred_element_type=jnp.float32) + fc1_bias
    hidden_act = gelu_tanh(hidden_pre).astype(jnp.bfloat16)
    mlp_branch = lax.psum_scatter(
        jnp.dot(hidden_act, fc2_weight, preferred_element_type=jnp.float32).astype(jnp.bfloat16),
        "mp",
        scatter_dimension=0,
        tiled=True,
    ).astype(jnp.float32)
    result = middle + (mlp_branch + fc2_bias) * row_live
    return (
        result,
        middle,
        rows_one,
        query_rows,
        key_rows,
        value_rows,
        bias_win,
        key_usable,
        log_total,
        head_out,
        rows_two,
        hidden_pre,
        hidden_act,
    )


def shards(
    tokens,
    crop_kind,
    norm1_gain,
    norm1_bias,
    qkv_weight,
    qv_bias,
    rel_table,
    proj_weight,
    proj_bias,
    norm2_gain,
    norm2_bias,
    fc1_weight,
    fc1_bias,
    fc2_weight,
    fc2_bias,
    out_grad,
):
    params = (
        norm1_gain,
        norm1_bias,
        qkv_weight,
        qv_bias,
        rel_table,
        proj_weight,
        proj_bias,
        norm2_gain,
        norm2_bias,
        fc1_weight,
        fc1_bias,
        fc2_weight,
        fc2_bias,
    )
    onehot = table_onehot()
    own_rows = tokens.shape[0]
    own_windows = own_rows // WIN
    own_kind = lax.dynamic_slice_in_dim(crop_kind, lax.axis_index("mp") * own_windows, own_windows)
    row_live = (
        (jnp.arange(WIN)[None, :] < window_live(own_kind)[:, None])
        .astype(jnp.float32)
        .reshape(own_rows, 1)
    )
    inputs = tokens.astype(jnp.float32)
    first_pass = forward_pass(inputs, crop_kind, row_live, params, onehot)
    block_out = first_pass[0].astype(jnp.bfloat16)
    saved = forward_pass(inputs, crop_kind, row_live, params, onehot)
    (
        unused_out,
        middle,
        rows_one,
        query_rows,
        key_rows,
        value_rows,
        bias_win,
        key_usable,
        log_total,
        head_out,
        rows_two,
        hidden_pre,
        hidden_act,
    ) = saved
    head_cols = qkv_weight.shape[2]
    heads_here = head_cols // HEAD
    windows = crop_kind.shape[0]
    win_shape = (windows, WIN, heads_here, HEAD)
    upstream = out_grad.astype(jnp.float32)
    mlp_grad = upstream * row_live
    fc2_bias_grad = jnp.sum(mlp_grad, axis=0)
    mlp_grad_rows = lax.all_gather(mlp_grad.astype(jnp.bfloat16), "mp", axis=0, tiled=True)
    fc2_weight_grad = dot_rows(hidden_act, mlp_grad_rows)
    act_grad = dot_back(mlp_grad_rows, fc2_weight)
    unused_act, gelu_pull = jax.vjp(gelu_tanh, hidden_pre)
    pre_grad = gelu_pull(act_grad)[0].astype(jnp.bfloat16)
    fc1_bias_grad = jnp.sum(pre_grad.astype(jnp.float32), axis=0)
    fc1_weight_grad = dot_rows(rows_two, pre_grad)
    normed_two_grad = lax.psum_scatter(
        dot_back(pre_grad, fc1_weight).astype(jnp.bfloat16), "mp", scatter_dimension=0, tiled=True
    ).astype(jnp.float32)
    unused_two, norm_two_pull = jax.vjp(normalize, middle, norm2_gain, norm2_bias)
    middle_grad, norm2_gain_grad, norm2_bias_grad = norm_two_pull(normed_two_grad)
    middle_grad = middle_grad + upstream
    attn_grad = middle_grad * row_live
    proj_bias_grad = jnp.sum(attn_grad, axis=0)
    attn_grad_rows = lax.all_gather(attn_grad.astype(jnp.bfloat16), "mp", axis=0, tiled=True)
    proj_weight_grad = dot_rows(head_out, attn_grad_rows)
    head_grad = dot_back(attn_grad_rows, proj_weight).astype(jnp.bfloat16).reshape(win_shape)
    query_four = query_rows.reshape(win_shape)
    key_four = key_rows.reshape(win_shape)
    scores = attention_scores(query_four, key_four, bias_win, key_usable)
    prob_full = jnp.exp(scores - log_total)
    prob_bf = prob_full.astype(jnp.bfloat16)
    prob_grad = jnp.einsum(
        "wqhd,wkhd->whqk",
        head_grad,
        value_rows.reshape(win_shape),
        preferred_element_type=jnp.float32,
    )
    value_grad = (
        jnp.einsum("whqk,wqhd->wkhd", prob_bf, head_grad, preferred_element_type=jnp.float32)
        .reshape(-1, head_cols)
        .astype(jnp.bfloat16)
    )
    score_grad = prob_full * (prob_grad - jnp.sum(prob_full * prob_grad, axis=-1, keepdims=True))
    is_global = (crop_kind == 0)[:, None, None, None]
    bias_grad = jnp.stack(
        [
            jnp.sum(jnp.where(is_global, score_grad, 0.0), axis=0),
            jnp.sum(jnp.where(is_global, 0.0, score_grad), axis=0),
        ]
    ).reshape(2, heads_here, WIN * WIN)
    rel_table_grad = jnp.einsum("kpt,khp->th", onehot, bias_grad, precision=HIGHEST)
    score_bf = score_grad.astype(jnp.bfloat16)
    query_grad = (
        jnp.einsum(
            "whqk,wkhd->wqhd", score_bf, key_four, preferred_element_type=jnp.float32
        ).reshape(-1, head_cols)
        * HEAD ** (-0.5)
    ).astype(jnp.bfloat16)
    key_grad = (
        jnp.einsum("whqk,wqhd->wkhd", score_bf, query_four, preferred_element_type=jnp.float32)
        .reshape(-1, head_cols)
        .astype(jnp.bfloat16)
    )
    qkv_weight_grad = jnp.stack(
        [
            dot_rows(rows_one, query_grad),
            dot_rows(rows_one, key_grad),
            dot_rows(rows_one, value_grad),
        ]
    )
    qv_bias_grad = jnp.stack(
        [
            jnp.sum(query_grad.astype(jnp.float32), axis=0),
            jnp.sum(value_grad.astype(jnp.float32), axis=0),
        ]
    )
    total = dot_back(query_grad, qkv_weight[0])
    total = total + dot_back(key_grad, qkv_weight[1])
    normed_one_grad = lax.psum_scatter(
        (total + dot_back(value_grad, qkv_weight[2])).astype(jnp.bfloat16),
        "mp",
        scatter_dimension=0,
        tiled=True,
    ).astype(jnp.float32)
    unused_one, norm_one_pull = jax.vjp(normalize, inputs, norm1_gain, norm1_bias)
    input_grad, norm1_gain_grad, norm1_bias_grad = norm_one_pull(normed_one_grad)
    tokens_grad = (input_grad + middle_grad).astype(jnp.bfloat16)
    small_grads = jnp.stack(
        [
            norm1_gain_grad,
            norm1_bias_grad,
            proj_bias_grad,
            norm2_gain_grad,
            norm2_bias_grad,
            fc2_bias_grad,
        ]
    )
    small_grads = lax.psum(small_grads, "mp")
    (
        qkv_weight_grad,
        qv_bias_grad,
        rel_table_grad,
        proj_weight_grad,
        fc1_weight_grad,
        fc1_bias_grad,
        fc2_weight_grad,
        small_grads,
    ) = (
        lax.psum(qkv_weight_grad.astype(jnp.bfloat16), "dp").astype(jnp.float32),
        lax.psum(qv_bias_grad.astype(jnp.bfloat16), "dp").astype(jnp.float32),
        lax.psum(rel_table_grad.astype(jnp.bfloat16), "dp").astype(jnp.float32),
        lax.psum(proj_weight_grad.astype(jnp.bfloat16), "dp").astype(jnp.float32),
        lax.psum(fc1_weight_grad.astype(jnp.bfloat16), "dp").astype(jnp.float32),
        lax.psum(fc1_bias_grad.astype(jnp.bfloat16), "dp").astype(jnp.float32),
        lax.psum(fc2_weight_grad.astype(jnp.bfloat16), "dp").astype(jnp.float32),
        lax.psum(small_grads.astype(jnp.bfloat16), "dp").astype(jnp.float32),
    )
    return (
        block_out,
        tokens_grad,
        small_grads[0],
        small_grads[1],
        qkv_weight_grad,
        qv_bias_grad,
        rel_table_grad,
        proj_weight_grad,
        small_grads[2],
        small_grads[3],
        small_grads[4],
        fc1_weight_grad,
        fc1_bias_grad,
        fc2_weight_grad,
        small_grads[5],
    )


def solution(mesh):
    in_specs = (
        P(("dp", "mp"), None),
        P("dp"),
        P(),
        P(),
        P(None, None, "mp"),
        P(None, "mp"),
        P(None, "mp"),
        P("mp", None),
        P(),
        P(),
        P(),
        P(None, "mp"),
        P("mp"),
        P("mp", None),
        P(),
        P(("dp", "mp"), None),
    )
    out_specs = (
        P(("dp", "mp"), None),
        P(("dp", "mp"), None),
        P(),
        P(),
        P(None, None, "mp"),
        P(None, "mp"),
        P(None, "mp"),
        P("mp", None),
        P(),
        P(),
        P(),
        P(None, "mp"),
        P("mp"),
        P("mp", None),
        P(),
    )
    return jax.shard_map(shards, mesh=mesh, in_specs=in_specs, out_specs=out_specs, check_vma=False)
```

profile of v0, /device:TPU:0, one launch (start us, length us, event | category | flops | bytes accessed | tf_op | source)
XLA Modules:
  0.0 543.4 jit_solution(10992987895275895568)
XLA Ops:
  16.2 44.7 %all-gather.9.cloned.1.call-done = bf16[8,147,768]{2,1,0:T(8,128)(2,1)} async-done(((bf16[1,147,768]{2,1,0:T(8,128)(2,1)}), bf16[8,147,768]{2,1,0:T(8,128)(2,1)}) %all-gather.9.cloned.1.call-update) | async-done | bytes 1806352 | tf_op jit(solution)/shard_map/all_gather | solution.py:83
  79.5 44.9 %fusion = bf16[152,768]{1,0:T(8,128)(2,1)S(1)} fusion(bf16[1176,768]{1,0:T(8,128)(2,1)} %convolution_convert_fusion.2), kind=kCustom, calls=%all-reduce-scatter | all-reduce-scatter fusion | flops 933889 | bytes 2040320
  127.8 2.8 concatenate.2
  134.3 47.2 %all-gather.13.cloned.1.call-done = bf16[8,147,768]{2,1,0:T(8,128)(2,1)} async-done(((bf16[1,147,768]{2,1,0:T(8,128)(2,1)}), bf16[8,147,768]{2,1,0:T(8,128)(2,1)}) %all-gather.13.cloned.1.call-update) | async-done | bytes 1806352 | tf_op jit(solution)/shard_map/all_gather | solution.py:220
  181.6 3.3 reshape.427
  184.9 4.0 fusion.98
  188.9 41.1 %all-gather.11.cloned.1.call-done = bf16[8,147,768]{2,1,0:T(8,128)(2,1)} async-done(((bf16[1,147,768]{2,1,0:T(8,128)(2,1)}), bf16[8,147,768]{2,1,0:T(8,128)(2,1)}) %all-gather.11.cloned.1.call-update) | async-done | bytes 1806352 | tf_op jit(solution)/shard_map/all_gather | solution.py:125
  230.0 3.4 reshape.425
  233.3 6.0 %fusion.91 = (bf16[384]{0:T(512)(128)(2,1)}, bf16[1176,384]{1,0:T(8,128)(2,1)S(1)}, f32[1176,384]{1,0:T(8,128)}) fusion(f32[1176,384]{1,0:T(8,128)} %fusion.98, f32[384]{0:T(512)S(1)} %copy-done.51, bf16[1176,768]{1,0:T(8,128)(2,1)} %reshape.425, bf16[768,384]{1,0:T(8,128)(2,1)S(1)} %copy-done), kind=kOutput, calls=%fused_computation.168 | convolution fusion | flops 703567488 | bytes 6914304 | tf_op jit(solution)/shard_map/dot_general | solution.py:126
  242.7 45.4 %fusion.2 = bf16[152,768]{1,0:T(8,128)(2,1)} fusion(bf16[1176,768]{1,0:T(8,128)(2,1)} %convolution_convert_fusion), kind=kCustom, calls=%all-reduce-scatter.2 | all-reduce-scatter fusion | flops 933889 | bytes 2040320
  292.0 4.0 concatenate.4
  300.9 3.9 convolution_convert_fusion.6
  304.8 2.7 convolution_convert_fusion.1
  311.7 37.9 %all-gather.15.cloned.1.call-done = bf16[8,147,768]{2,1,0:T(8,128)(2,1)} async-done(((bf16[1,147,768]{2,1,0:T(8,128)(2,1)}), bf16[8,147,768]{2,1,0:T(8,128)(2,1)}) %all-gather.15.cloned.1.call-update) | async-done | bytes 1806352 | tf_op jit(solution)/shard_map/all_gather | solution.py:235
  349.7 3.4 reshape.429
  353.0 2.8 convolution_convert_fusion.10
  359.6 3.3 fusion.96
  370.9 3.4 fusion.68
  387.1 2.7 convolution_add_fusion.1
  390.5 76.4 %fusion.90 = (bf16[152,768]{1,0:T(8,128)(2,1)S(1)}, bf16[152,768]{1,0:T(8,128)(2,1)S(1)}) fusion(bf16[1176,768]{1,0:T(8,128)(2,1)} %convolution_convert_fusion.1, bf16[1176,768]{1,0:T(8,128)(2,1)S(1)} %fusion.6), kind=kCustom, calls=%all-reduce-scatter.4 | all-reduce-scatter fusion | flops 1867777 | bytes 4080128
  467.0 3.4 collective-permute-start.3
  470.5 4.5 collective-permute-start.1
  480.6 35.2 %psum.63 = bf16[6,768]{1,0:T(8,128)(2,1)S(1)} all-reduce(f32[6,768]{1,0:T(8,128)S(1)} %stack.58), channel_id=1, replica_groups=mesh['dp'=4,'mp'=8] {'mp'}, use_global_device_ids=true, to_apply=%region_21.22 | all-reduce | flops 4608 | bytes 27648 | tf_op jit(solution)/shard_map/psum | solution.py:309
  515.8 10.7 %all-reduce.8 = (bf16[6,768]{1,0:T(8,128)(2,1)S(1)}, bf16[2,96]{1,0:T(2,128)(2,1)S(1)}, bf16[169,3]{0,1:T(4,128)(2,1)S(1)}, bf16[384]{0:T(512)(128)(2,1)S(1)}) all-reduce(bf16[6,768]{1,0:T(8,128)(2,1)S(1)} %psum.63, bf16[2,96]{1,0:T(2,128)(2,1)S(1)} %pad_maximum_fusion.1, ...), channel_id=1, replica_groups=mesh['dp'=4,'mp'=8] {'dp'}, use_global_device_ids=true, to_apply=%region_22.23 | all-reduce | flops 5691 | bytes 22764 | tf_op jit(solution)/shard_map/psum | solution.py:327
  (251 shorter events, 90.7 us)
Async XLA Ops:
  7.2 226.1 %copy-start = (bf16[768,384]{1,0:T(8,128)(2,1)S(1)}, bf16[768,384]{1,0:T(8,128)(2,1)}, u32[]{:S(2)}) copy-start(bf16[768,384]{1,0:T(8,128)(2,1)} %param.27) | copy-start | bytes 1769476
  7.2 53.6 %all-gather.9.cloned.1.call-start = ((), (), s32[]{:S(2)}) async-start(), calls=%async_computation | async-start | bytes 2101248 | tf_op jit(solution)/shard_map/all_gather | solution.py:83
  11.4 170.1 %all-gather.13.cloned.1.call-start = ((), (), s32[]{:S(2)}) async-start(), calls=%async_computation.2 | async-start | bytes 2101248 | tf_op jit(solution)/shard_map/all_gather | solution.py:220
  16.1 54.7 %copy-start.46 = (pred[24]{0:T(512)(128)(4,1)}, pred[24]{0:T(512)(128)(4,1)S(1)}, u32[]{:S(2)}) copy-start(pred[24]{0:T(512)(128)(4,1)S(1)} %broadcast_compare_fusion) | copy-start | bytes 76
  16.2 46.7 %copy-start.20 = (bf16[3,768,96]{1,2,0:T(8,128)(2,1)S(1)}, bf16[3,768,96]{1,2,0:T(8,128)(2,1)}, u32[]{:S(2)}) copy-start(bf16[3,768,96]{1,2,0:T(8,128)(2,1)} %param.20) | copy-start | bytes 1327108
  77.6 48.9 %copy-start.48 = (u32[32]{0:T(128)S(1)}, u32[32]{0:T(128)}, u32[]{:S(2)}) copy-start(u32[32]{0:T(128)} %constant.105) | copy-start | bytes 388
  79.5 51.1 %copy-start.3 = (bf16[147,768]{1,0:T(8,128)(2,1)S(1)}, bf16[147,768]{1,0:T(8,128)(2,1)}, u32[]{:S(2)}) copy-start(bf16[147,768]{1,0:T(8,128)(2,1)} %param.16) | copy-start | bytes 677380
  79.5 51.1 %copy-start.29 = (f32[768]{0:T(1024)S(1)}, f32[768]{0:T(1024)}, u32[]{:S(2)}) copy-start(f32[768]{0:T(1024)} %param.24) | copy-start | bytes 9220
  79.5 53.3 %copy-start.32 = (f32[768]{0:T(1024)S(1)}, f32[768]{0:T(1024)}, u32[]{:S(2)}) copy-start(f32[768]{0:T(1024)} %param.25) | copy-start | bytes 9220
  79.5 53.3 %copy-start.42 = (f32[768]{0:T(1024)S(1)}, f32[768]{0:T(1024)}, u32[]{:S(2)}) copy-start(f32[768]{0:T(1024)} %param.26) | copy-start | bytes 9220
  124.4 3.3 collective-permute-start
  132.8 97.2 %all-gather.11.cloned.1.call-start = ((), (), s32[]{:S(2)}) async-start(), calls=%async_computation.1 | async-start | bytes 2101248 | tf_op jit(solution)/shard_map/all_gather | solution.py:125
  133.8 215.8 %all-gather.15.cloned.1.call-start = ((), (), s32[]{:S(2)}) async-start(), calls=%async_computation.3 | async-start | bytes 2101248 | tf_op jit(solution)/shard_map/all_gather | solution.py:235
  188.9 44.4 %copy-start.51 = (f32[384]{0:T(512)S(1)}, f32[384]{0:T(512)}, u32[]{:S(2)}) copy-start(f32[384]{0:T(512)} %param.28) | copy-start | bytes 4612
  288.9 3.1 collective-permute-start.2
  300.7 230.0 %all-reduce.13.cloned.1.call-start = ((), (), s32[]{:S(2)}) async-start(), calls=%async_computation.4 | async-start | bytes 3538944 | tf_op jit(solution)/shard_map/psum | solution.py:320
  390.5 86.9 %copy-start.25 = (bf16[1,768,96]{1,2,0:T(8,128)(2,1)S(1)}, bf16[1,768,96]{1,2,0:T(8,128)(2,1)}, u32[]{:S(2)}) copy-start(bf16[1,768,96]{1,2,0:T(8,128)(2,1)} %fusion.26) | copy-start | bytes 442372
  467.0 12.3 %collective-permute-start.3 = (bf16[35,768]{1,0:T(8,128)(2,1)S(1)}, bf16[35,768]{1,0:T(8,128)(2,1)S(1)}, u32[]{:S(2)}, u32[]{:S(2)}) collective-permute-start(bf16[35,768]{1,0:T(8,128)(2,1)S(1)} %slice.75), channel_id=1, source_target_pairs={{0,1},{1,2},{2,3},{3,4},{4,5},{5,6},{6,7},{8,9},{9,10},{10,11},{11... | collective-permute-start | bytes 161288
  470.5 57.8 %collective-permute-start.1 = (bf16[35,768]{1,0:T(8,128)(2,1)S(1)}, bf16[35,768]{1,0:T(8,128)(2,1)S(1)}, u32[]{:S(2)}, u32[]{:S(2)}) collective-permute-start(bf16[35,768]{1,0:T(8,128)(2,1)S(1)} %slice.73), channel_id=1, source_target_pairs={{0,1},{1,2},{2,3},{3,4},{4,5},{5,6},{6,7},{8,9},{9,10},{10,11},{11... | collective-permute-start | bytes 161288
  479.2 36.6 %copy-start.44 = (bf16[384]{0:T(512)(128)(2,1)S(1)}, bf16[384]{0:T(512)(128)(2,1)}, u32[]{:S(2)}) copy-start(bf16[384]{0:T(512)(128)(2,1)} %get-tuple-element.43) | copy-start | bytes 2308
  479.3 50.1 %copy-start.7 = (f32[147,768]{1,0:T(8,128)S(1)}, f32[147,768]{1,0:T(8,128)}, u32[]{:S(2)}) copy-start(f32[147,768]{1,0:T(8,128)} %copy-done.6) | copy-start | bytes 1354756
  479.3 50.1 %copy-start.16 = (bf16[147,768]{1,0:T(8,128)(2,1)S(1)}, bf16[147,768]{1,0:T(8,128)(2,1)}, u32[]{:S(2)}) copy-start(bf16[147,768]{1,0:T(8,128)(2,1)} %param.31) | copy-start | bytes 677380
  479.3 50.1 %copy-start.39 = (f32[147]{0:T(256)S(1)}, f32[147]{0:T(256)}, u32[]{:S(2)}) copy-start(f32[147]{0:T(256)} %copy-done.38) | copy-start | bytes 1768
  479.3 50.1 %copy-start.43 = (f32[768]{0:T(1024)S(1)}, f32[768]{0:T(1024)}, u32[]{:S(2)}) copy-start(f32[768]{0:T(1024)} %param.30) | copy-start | bytes 9220
  (42 other events, 143.8 us)
Sparse Core Ops, SparseCore 0:
  11.6 49.2 all-gather.8
  132.9 48.6 all-gather.12
  184.3 45.5 all-gather.10
  300.8 48.8 all-gather.14
  479.5 45.8 all-reduce.12
where the time goes:
time: 553 us; the launch traced here: 543 us
  blocking collectives  213 us (39%)
  waiting for transfers between devices  172 us (31%)
  matrix products  56.3 us (10%)
  local copies, waits for them, and re-layouts  49.3 us (9%)
  other arithmetic  24.9 us (5%)
  between operations  15.5 us (3%)
  starting transfers between devices  12.6 us (2%)
    unnamed x3, blocking collectives  167 us
    all_gather x1, waiting for transfers between devices, shards(): lax.all_gather(mlp_grad.astype(jnp.bfloat16), 'mp', axis=0, tiled=True)  47.2 us
    all_gather x1, waiting for transfers between devices, forward_pass(): rows_one = lax.all_gather(normed_one, 'mp', axis=0, tiled=True)  44.7 us
    all_gather x1, waiting for transfers between devices, forward_pass(): rows_two = lax.all_gather(normed_two, 'mp', axis=0, tiled=True)  41.1 us
    all_gather x1, waiting for transfers between devices, shards(): lax.all_gather(attn_grad.astype(jnp.bfloat16), 'mp', axis=0, tiled=True)  37.9 us
    psum x1, blocking collectives, shards(): small_grads = lax.psum(small_grads, 'mp')  35.2 us
    unnamed x128, local copies, waits for them, and re-layouts  24.7 us
    dot_general x6, matrix products, dot_rows(): lax.dot_general(left, right, (((0,), (0,)), ((), ())), preferred_element_...  15.2 us
  transfers between devices with their start and end apart: 9, of which 5 were waited for; matrix products, arithmetic and copies ran while one was open for 6% of the time, Pallas kernels for 0%

commit v1 on v0

--- a/solution.py
+++ b/solution.py
@@ -306,7 +306,15 @@
             fc2_bias_grad,
         ]
     )
-    small_grads = lax.psum(small_grads, "mp")
+    y2, later = (small_grads, 0)
+    wide_n = jax.lax.axis_size("mp")
+    while 1 << later < wide_n:
+        local_part = jax.lax.ppermute(
+            y2, axis_name="mp", perm=[(t, t ^ 1 << later) for t in range(wide_n)]
+        )
+        y2 = y2 + local_part
+        later = later + 1
+    small_grads = y2
     (
         qkv_weight_grad,
         qv_bias_grad,

time: 553 us -> 546 us (0.987)
  blocking collectives: 213 us -> 178 us
  waiting for transfers between devices: 172 us -> 199 us
    psum x1 -> x0, blocking collectives: 35.2 us -> none  [shards(): small_grads = lax.psum(small_grads, 'mp')]
    psum x1, waiting for transfers between devices: 0.01 us -> 18.4 us  [shards(): lax.psum(qkv_weight_grad.astype(jnp.bfloat16), 'dp').astype(jnp.float32)]
    ppermute x0 -> x3, waiting for transfers between devices: none -> 8.23 us  [shards(): jax.lax.ppermute(y2, axis_name='mp', perm=[(t, t ^ 1 << later) for t in r...]
    unnamed x128 -> x130, local copies, waits for them, and re-layouts: 24.7 us -> 24.8 us
  transfers between devices with their start and end apart: 9 -> 12, of which waited for: 5 -> 9; matrix products, arithmetic and copies ran while one was open for 6% -> 6% of each run, Pallas kernels for 0% -> 0%
where the time goes in v1:
time: 546 us; the launch traced here: 537 us
  waiting for transfers between devices  199 us (36%)
  blocking collectives  178 us (33%)
  matrix products  56.8 us (10%)
  local copies, waits for them, and re-layouts  47.8 us (9%)
  other arithmetic  24.9 us (5%)
  starting transfers between devices  15.6 us (3%)
  between operations  15.5 us (3%)
    unnamed x3, blocking collectives  167 us
    all_gather x1, waiting for transfers between devices, shards(): lax.all_gather(mlp_grad.astype(jnp.bfloat16), 'mp', axis=0, tiled=True)  47.2 us
    all_gather x1, waiting for transfers between devices, forward_pass(): rows_one = lax.all_gather(normed_one, 'mp', axis=0, tiled=True)  44.7 us
    all_gather x1, waiting for transfers between devices, forward_pass(): rows_two = lax.all_gather(normed_two, 'mp', axis=0, tiled=True)  41.1 us
    all_gather x1, waiting for transfers between devices, shards(): lax.all_gather(attn_grad.astype(jnp.bfloat16), 'mp', axis=0, tiled=True)  37.9 us
    unnamed x130, local copies, waits for them, and re-layouts  24.8 us
    psum x1, waiting for transfers between devices, shards(): lax.psum(qkv_weight_grad.astype(jnp.bfloat16), 'dp').astype(jnp.float32)  18.4 us
    dot_general x6, matrix products, dot_rows(): lax.dot_general(left, right, (((0,), (0,)), ((), ())), preferred_element_...  15.2 us
  transfers between devices with their start and end apart: 12, of which 9 were waited for; matrix products, arithmetic and copies ran while one was open for 6% of the time, Pallas kernels for 0%

profile of v1, /device:TPU:0, one launch (start us, length us, event | category | flops | bytes accessed | tf_op | source)
XLA Modules:
  0.0 537.0 jit_solution(2150522789064452648)
XLA Ops:
  16.2 44.7 %all-gather.9.cloned.1.call-done = bf16[8,147,768]{2,1,0:T(8,128)(2,1)} async-done(((bf16[1,147,768]{2,1,0:T(8,128)(2,1)}), bf16[8,147,768]{2,1,0:T(8,128)(2,1)}) %all-gather.9.cloned.1.call-update) | async-done | bytes 1806352 | tf_op jit(solution)/shard_map/all_gather | solution.py:83
  79.5 44.9 %fusion = bf16[152,768]{1,0:T(8,128)(2,1)S(1)} fusion(bf16[1176,768]{1,0:T(8,128)(2,1)} %convolution_convert_fusion.2), kind=kCustom, calls=%all-reduce-scatter | all-reduce-scatter fusion | flops 933889 | bytes 2040320
  127.8 2.8 concatenate.2
  134.3 47.2 %all-gather.13.cloned.1.call-done = bf16[8,147,768]{2,1,0:T(8,128)(2,1)} async-done(((bf16[1,147,768]{2,1,0:T(8,128)(2,1)}), bf16[8,147,768]{2,1,0:T(8,128)(2,1)}) %all-gather.13.cloned.1.call-update) | async-done | bytes 1806352 | tf_op jit(solution)/shard_map/all_gather | solution.py:220
  181.6 3.3 reshape.427
  184.9 4.0 fusion.98
  188.9 41.1 %all-gather.11.cloned.1.call-done = bf16[8,147,768]{2,1,0:T(8,128)(2,1)} async-done(((bf16[1,147,768]{2,1,0:T(8,128)(2,1)}), bf16[8,147,768]{2,1,0:T(8,128)(2,1)}) %all-gather.11.cloned.1.call-update) | async-done | bytes 1806352 | tf_op jit(solution)/shard_map/all_gather | solution.py:125
  229.9 3.4 reshape.425
  233.3 6.0 %fusion.91 = (bf16[384]{0:T(512)(128)(2,1)}, bf16[1176,384]{1,0:T(8,128)(2,1)S(1)}, f32[1176,384]{1,0:T(8,128)}) fusion(f32[1176,384]{1,0:T(8,128)} %fusion.98, f32[384]{0:T(512)S(1)} %copy-done.53, bf16[1176,768]{1,0:T(8,128)(2,1)} %reshape.425, bf16[768,384]{1,0:T(8,128)(2,1)S(1)} %copy-done), kind=kOutput, calls=%fused_computation.169 | convolution fusion | flops 703567488 | bytes 6914304 | tf_op jit(solution)/shard_map/dot_general | solution.py:126
  242.6 45.4 %fusion.2 = bf16[152,768]{1,0:T(8,128)(2,1)} fusion(bf16[1176,768]{1,0:T(8,128)(2,1)} %convolution_convert_fusion), kind=kCustom, calls=%all-reduce-scatter.2 | all-reduce-scatter fusion | flops 933889 | bytes 2040320
  292.0 4.0 concatenate.4
  300.9 3.9 convolution_convert_fusion.6
  311.7 37.9 %all-gather.15.cloned.1.call-done = bf16[8,147,768]{2,1,0:T(8,128)(2,1)} async-done(((bf16[1,147,768]{2,1,0:T(8,128)(2,1)}), bf16[8,147,768]{2,1,0:T(8,128)(2,1)}) %all-gather.15.cloned.1.call-update) | async-done | bytes 1806352 | tf_op jit(solution)/shard_map/all_gather | solution.py:235
  349.6 3.4 reshape.429
  353.0 2.8 convolution_convert_fusion.10
  359.6 3.9 fusion.96
  371.4 3.5 fusion.68
  389.5 76.4 %fusion.90 = (bf16[152,768]{1,0:T(8,128)(2,1)S(1)}, bf16[152,768]{1,0:T(8,128)(2,1)S(1)}) fusion(bf16[1176,768]{1,0:T(8,128)(2,1)} %convolution_convert_fusion.1, bf16[1176,768]{1,0:T(8,128)(2,1)S(1)} %fusion.6), kind=kCustom, calls=%all-reduce-scatter.4 | all-reduce-scatter fusion | flops 1867777 | bytes 4080128
  465.9 3.4 collective-permute-start.6
  469.4 4.5 collective-permute-start.4
  484.7 2.8 collective-permute-done.1
  489.0 3.6 collective-permute-done.2
  492.6 11.0 %all-reduce.8 = (bf16[6,768]{1,0:T(8,128)(2,1)S(1)}, bf16[2,96]{1,0:T(2,128)(2,1)S(1)}, bf16[169,3]{0,1:T(4,128)(2,1)S(1)}, bf16[384]{0:T(512)(128)(2,1)S(1)}) all-reduce(bf16[6,768]{1,0:T(8,128)(2,1)S(1)} %add_convert_fusion.3, bf16[2,96]{1,0:T(2,128)(2,1)S(1)} %pad_maximum_fusion.1, ...), channel_id=1, replica_groups=mesh['dp'=4,'mp'=8] {'dp'}, use_global_device_ids=true, to_apply=%region_21.22 | all-reduce | flops 5691 | bytes 22764 | tf_op jit(solution)/shard_map/psum | solution.py:335
  505.9 18.4 %all-reduce.13.cloned.1.call-done = (bf16[3,768,96]{1,2,0:T(8,128)(2,1)}, bf16[96,768]{1,0:T(8,128)(2,1)}, bf16[768,384]{1,0:T(8,128)(2,1)}, bf16[384,768]{1,0:T(8,128)(2,1)}) async-done(((bf16[3,768,96]{1,2,0:T(8,128)(2,1)}, bf16[96,768]{1,0:T(8,128)(2,1)}, bf16[768,384]{1,0:T(8,128)(2,1)}, bf16[384,768]{1,0:T(8,128)(2,1)}), (bf16[3,768,96]{1,2,0:T(8,128)(2,1)}, bf16[96,768]{1,0:T(8,128)(2,1)}, ...) | async-done | bytes 1769488 | tf_op jit(solution)/shard_map/psum | solution.py:328
  (261 shorter events, 99.3 us)
Async XLA Ops:
  7.2 226.1 %copy-start = (bf16[768,384]{1,0:T(8,128)(2,1)S(1)}, bf16[768,384]{1,0:T(8,128)(2,1)}, u32[]{:S(2)}) copy-start(bf16[768,384]{1,0:T(8,128)(2,1)} %param.27) | copy-start | bytes 1769476
  7.2 53.6 %all-gather.9.cloned.1.call-start = ((), (), s32[]{:S(2)}) async-start(), calls=%async_computation | async-start | bytes 2101248 | tf_op jit(solution)/shard_map/all_gather | solution.py:83
  11.4 170.1 %all-gather.13.cloned.1.call-start = ((), (), s32[]{:S(2)}) async-start(), calls=%async_computation.2 | async-start | bytes 2101248 | tf_op jit(solution)/shard_map/all_gather | solution.py:220
  16.1 54.7 %copy-start.48 = (pred[24]{0:T(512)(128)(4,1)}, pred[24]{0:T(512)(128)(4,1)S(1)}, u32[]{:S(2)}) copy-start(pred[24]{0:T(512)(128)(4,1)S(1)} %broadcast_compare_fusion) | copy-start | bytes 76
  16.2 46.7 %copy-start.21 = (bf16[3,768,96]{1,2,0:T(8,128)(2,1)S(1)}, bf16[3,768,96]{1,2,0:T(8,128)(2,1)}, u32[]{:S(2)}) copy-start(bf16[3,768,96]{1,2,0:T(8,128)(2,1)} %param.20) | copy-start | bytes 1327108
  77.6 48.9 %copy-start.50 = (u32[32]{0:T(128)S(1)}, u32[32]{0:T(128)}, u32[]{:S(2)}) copy-start(u32[32]{0:T(128)} %constant.105) | copy-start | bytes 388
  79.5 51.1 %copy-start.3 = (bf16[147,768]{1,0:T(8,128)(2,1)S(1)}, bf16[147,768]{1,0:T(8,128)(2,1)}, u32[]{:S(2)}) copy-start(bf16[147,768]{1,0:T(8,128)(2,1)} %param.16) | copy-start | bytes 677380
  79.5 51.1 %copy-start.30 = (f32[768]{0:T(1024)S(1)}, f32[768]{0:T(1024)}, u32[]{:S(2)}) copy-start(f32[768]{0:T(1024)} %param.24) | copy-start | bytes 9220
  79.5 53.3 %copy-start.33 = (f32[768]{0:T(1024)S(1)}, f32[768]{0:T(1024)}, u32[]{:S(2)}) copy-start(f32[768]{0:T(1024)} %param.25) | copy-start | bytes 9220
  79.5 53.3 %copy-start.43 = (f32[768]{0:T(1024)S(1)}, f32[768]{0:T(1024)}, u32[]{:S(2)}) copy-start(f32[768]{0:T(1024)} %param.26) | copy-start | bytes 9220
  124.4 3.3 collective-permute-start.3
  132.8 97.2 %all-gather.11.cloned.1.call-start = ((), (), s32[]{:S(2)}) async-start(), calls=%async_computation.1 | async-start | bytes 2101248 | tf_op jit(solution)/shard_map/all_gather | solution.py:125
  133.8 215.8 %all-gather.15.cloned.1.call-start = ((), (), s32[]{:S(2)}) async-start(), calls=%async_computation.3 | async-start | bytes 2101248 | tf_op jit(solution)/shard_map/all_gather | solution.py:235
  188.9 44.4 %copy-start.53 = (f32[384]{0:T(512)S(1)}, f32[384]{0:T(512)}, u32[]{:S(2)}) copy-start(f32[384]{0:T(512)} %param.28) | copy-start | bytes 4612
  288.8 3.1 collective-permute-start.5
  300.6 223.7 %all-reduce.13.cloned.1.call-start = ((), (), s32[]{:S(2)}) async-start(), calls=%async_computation.4 | async-start | bytes 3538944 | tf_op jit(solution)/shard_map/psum | solution.py:328
  389.4 86.9 %copy-start.26 = (bf16[1,768,96]{1,2,0:T(8,128)(2,1)S(1)}, bf16[1,768,96]{1,2,0:T(8,128)(2,1)}, u32[]{:S(2)}) copy-start(bf16[1,768,96]{1,2,0:T(8,128)(2,1)} %fusion.26) | copy-start | bytes 442372
  465.9 12.3 %copy-start.45 = (bf16[3,32]{1,0:T(4,128)(2,1)S(1)}, bf16[3,32]{1,0:T(4,128)(2,1)}, u32[]{:S(2)}) copy-start(bf16[3,32]{1,0:T(4,128)(2,1)} %get-tuple-element.62) | copy-start | bytes 580
  465.9 12.3 %collective-permute-start.6 = (bf16[35,768]{1,0:T(8,128)(2,1)S(1)}, bf16[35,768]{1,0:T(8,128)(2,1)S(1)}, u32[]{:S(2)}, u32[]{:S(2)}) collective-permute-start(bf16[35,768]{1,0:T(8,128)(2,1)S(1)} %slice.75), channel_id=1, source_target_pairs={{0,1},{1,2},{2,3},{3,4},{4,5},{5,6},{6,7},{8,9},{9,10},{10,11},{11... | collective-permute-start | bytes 161288
  469.4 15.0 %collective-permute-start.4 = (bf16[35,768]{1,0:T(8,128)(2,1)S(1)}, bf16[35,768]{1,0:T(8,128)(2,1)S(1)}, u32[]{:S(2)}, u32[]{:S(2)}) collective-permute-start(bf16[35,768]{1,0:T(8,128)(2,1)S(1)} %slice.73), channel_id=1, source_target_pairs={{0,1},{1,2},{2,3},{3,4},{4,5},{5,6},{6,7},{8,9},{9,10},{10,11},{11... | collective-permute-start | bytes 161288
  479.0 13.6 %copy-start.46 = (bf16[384]{0:T(512)(128)(2,1)S(1)}, bf16[384]{0:T(512)(128)(2,1)}, u32[]{:S(2)}) copy-start(bf16[384]{0:T(512)(128)(2,1)} %get-tuple-element.43) | copy-start | bytes 2308
  479.5 4.2 collective-permute-start
  483.7 3.8 collective-permute-start.1
  487.6 5.0 collective-permute-start.2
  (46 other events, 165.9 us)
Sparse Core Ops, SparseCore 0:
  11.6 49.2 all-gather.8
  132.9 48.6 all-gather.12
  184.3 45.5 all-gather.10
  300.7 48.8 all-gather.14
  478.4 45.8 all-reduce.12
